TPU v7x, 32 devices: a whole 2x2x4 slice. The times are simulated.
32 devices in a mesh: groups: 2 (over y), row: 8 (over z, x), col: 2 (over core).
Axes of the slice: x: 2, y: 2, z: 4, core: 2. Of those that a mesh axis runs over, the one named last changes fastest.
Arguments:
- first_counts: bfloat16 [4, 16, 262144], P('groups', None, ('row', 'col')), parts along dimension 0, may hold values from 1 to 100
- depth: int32 [4, 16, 262144], P('groups', None, ('row', 'col')), parts along dimension 0, may hold values from 6 to 8
- sources: int32 [4, 16], P('groups'), parts along dimension 0, may hold values from 0 to 262143
- tile_pos: int32 [16, 2, 48], P(('groups', 'row'), 'col'), parts along dimension 0, may hold values from 0 to 16383, as said below
- tile_live: int32 [16, 2], P(('groups', 'row'), 'col'), parts along dimension 0, may hold values from 6 to 48, as said below
- tile_bits: int32 [16, 2, 48, 64, 512], P(('groups', 'row'), 'col'), parts along dimension 0, may hold values from 0 to 255, as said below
Outputs:
- dependency: float32 [4, 16, 262144], P('groups', None, ('row', 'col')), parts along dimension 0
- centrality: float32 [524288], P(('groups', 'row', 'col')), parts along dimension 0
There are 2 independent parts, one for each index of `groups`. A program takes and returns all parts, laid end to end along the dimension named above; each array names one. Nothing has to cross between parts.
Inputs may be any that keep to these rules, and one draw needn't show every extreme that they name: The first tile_live[r, c] slots of device (r, c) hold its tiles, the rest are ignored; some device of each draw uses all 48 slots. `tile_pos`: among the 48 slots of one device, at most 6 have column blocks owned by any one device of its grid column; in every draw each grid column has a device that owns the column blocks of exactly 6 live slots of every device of that column. `tile_bits`: packed 0/1 adjacency words of 8 bits.
All inputs are finite; a program needn't handle non-finite values.
Results may differ from a plain program's by a relative error of at most 0.0011.
Values may be sent and summed in bfloat16 or wider, within the bound.
A program may use at most 128 MiB of HBM per device.

v0:
```python
import functools

import jax
import jax.numpy as jnp
from jax import lax
from jax.experimental import pallas as pl
from jax.experimental.pallas import tpu as pltpu
from jax.sharding import PartitionSpec as P

DEPTH = 8
STEPS = 2000.0
CODE_ZERO = -32768
MESH = pl.DeviceIdType.MESH


def encode(values):
    code = (jnp.log2(jnp.maximum(values, 1.0)) * STEPS + 0.5).astype(jnp.int32) + (CODE_ZERO + 1)
    return jnp.where(values > 0.0, code, CODE_ZERO).astype(jnp.int16)


def decode(code):
    wide = code.astype(jnp.int32)
    value = jnp.exp2((wide - (CODE_ZERO + 1)).astype(jnp.float32) * (1.0 / STEPS))
    return jnp.where(wide > CODE_ZERO, value, 0.0)


def unpack(words):
    count, width = words.shape
    shifts = lax.broadcasted_iota(jnp.int32, (count, 8, width), 1)
    bits = jnp.bitwise_and(jnp.right_shift(words[:, None, :], shifts), 1)
    return bits.reshape(count * 8, width).astype(jnp.float32).astype(jnp.bfloat16)


def loop(count, body):
    def step(index, carry):
        body(index)
        return carry

    lax.fori_loop(0, count, step, 0)


def kernel(
    layout,
    rows,
    cols,
    most,
    blocks,
    table,
    words,
    first,
    depth,
    sources,
    dependency,
    centrality,
    stripe0,
    stripe1,
    code_out,
    code_in0,
    code_in1,
    weight_out,
    weight_in0,
    weight_in1,
    weights,
    counts1,
    delta1,
    running,
    terms,
    sum_out,
    sum_in,
    code_sent,
    code_got,
    weight_sent,
    weight_got,
    stripe_sent,
    stripe_got,
    sum_sent,
    sum_got,
):
    seats = rows * most
    tile = words.shape[-1]
    stripe = (stripe0, stripe1)
    code_in = (code_in0, code_in1)
    weight_in = (weight_in0, weight_in1)
    row = lax.axis_index("row")
    col = lax.axis_index("col")
    partner = 1 - col

    def entry(name, index):
        return table[layout[name] + index]

    barrier = pltpu.get_barrier_semaphore()

    def greet(step):
        peer = lax.rem(row + step + 1, rows)
        pl.semaphore_signal(barrier, inc=1, device_id={"row": peer}, device_id_type=MESH)

    loop(rows - 1, greet)
    pl.semaphore_signal(barrier, inc=1, device_id={"col": partner}, device_id_type=MESH)

    def lanes(block):
        return pl.ds(pl.multiple_of(block * tile, tile), tile)

    def tile_of(seat):
        return unpack(jnp.bitwise_and(words[entry("slot", seat)], entry("fill", seat)))

    def stripe_copy(level):
        own = pl.ds(col * blocks, blocks)
        return pltpu.make_async_remote_copy(
            src_ref=stripe[level].at[own],
            dst_ref=stripe[level].at[own],
            send_sem=stripe_sent.at[level],
            recv_sem=stripe_got.at[level],
            device_id={"col": partner},
            device_id_type=MESH,
        )

    def stripe_arrival(level):
        other = pl.ds(partner * blocks, blocks)
        return pltpu.make_async_remote_copy(
            src_ref=stripe[level].at[other],
            dst_ref=stripe[level].at[other],
            send_sem=stripe_sent.at[level],
            recv_sem=stripe_got.at[level],
            device_id={"col": partner},
            device_id_type=MESH,
        )

    def seat_copy(out, into, sent, got, level, src_row, dst_row, peer):
        return pltpu.make_async_remote_copy(
            src_ref=out.at[level, pl.ds(dst_row * most, most)],
            dst_ref=into[level].at[pl.ds(src_row * most, most)],
            send_sem=sent.at[level, dst_row],
            recv_sem=got.at[level, src_row],
            device_id={"row": peer},
            device_id_type=MESH,
        )

    def leaving(step):
        return lax.rem(row + step + 1, rows)

    def arriving(step):
        return lax.rem(row + rows - 1 - step, rows)

    def segment_sums(load, order, same):
        def step(index, total):
            carry = total * entry(same, index).astype(jnp.float32)
            total = load(entry(order, index)) + carry
            running[index] = total
            return total

        lax.fori_loop(0, seats, step, jnp.zeros(running.shape[1:], jnp.float32))

    def segment(last, some, block):
        return running[entry(last, block)] * entry(some, block).astype(jnp.float32)

    def forward_level(level, finish):
        stripe_arrival(level).wait_recv()

        def product(seat):
            piece = stripe[level][entry("row", seat)]
            return encode(jnp.dot(piece, tile_of(seat), preferred_element_type=jnp.float32))

        def send(step):
            peer = leaving(step)

            def one(place):
                code_out[level, peer * most + place] = product(peer * most + place)

            loop(most, one)
            seat_copy(code_out, code_in, code_sent, code_got, level, row, peer, peer).start()

        loop(rows - 1, send)

        def own(place):
            code_in[level][row * most + place] = product(row * most + place)

        loop(most, own)

        def arrive(step):
            peer = arriving(step)
            seat_copy(code_out, code_in, code_sent, code_got, level, peer, row, peer).wait_recv()

        loop(rows - 1, arrive)
        segment_sums(lambda seat: decode(code_in[level][seat]), "in_order", "in_same")
        loop(blocks, lambda block: finish(block, segment("in_last", "in_some", block)))

    def backward_level(level, finish):
        def send(step):
            peer = leaving(step)

            def one(place):
                seat = peer * most + place
                weight_out[level, seat] = weights[level, entry("block", seat)]

            loop(most, one)
            seat_copy(weight_out, weight_in, weight_sent, weight_got, level, row, peer, peer).start()

        loop(rows - 1, send)

        def product(seat, piece):
            terms[seat] = lax.dot_general(
                piece, tile_of(seat), (((1,), (1,)), ((), ())), preferred_element_type=jnp.float32
            )

        def own(place):
            seat = row * most + place
            product(seat, weights[level, entry("block", seat)])

        loop(most, own)

        def arrive(step):
            peer = arriving(step)
            seat_copy(
                weight_out, weight_in, weight_sent, weight_got, level, peer, row, peer
            ).wait_recv()

            def one(place):
                seat = peer * most + place
                product(seat, weight_in[level][seat])

            loop(most, one)

        loop(rows - 1, arrive)
        segment_sums(lambda seat: terms[seat], "row_order", "row_same")

        def leave(block):
            sum_out[level, block] = segment("row_last", "row_some", partner * blocks + block)

        loop(blocks, leave)
        copy = pltpu.make_async_remote_copy(
            src_ref=sum_out.at[level],
            dst_ref=sum_in.at[level],
            send_sem=sum_sent.at[level],
            recv_sem=sum_got.at[level],
            device_id={"col": partner},
            device_id_type=MESH,
        )
        copy.start()
        copy.wait_recv()

        def total(block):
            mine = segment("row_last", "row_some", col * blocks + block)
            finish(block, mine + sum_in[level, block])

        loop(blocks, total)
        copy.wait_send()

    def start0(block):
        counts0 = first[:, lanes(block)].astype(jnp.float32)
        masked = jnp.where(depth[:, lanes(block)] == DEPTH - 2, counts0, 0.0)
        stripe0[col * blocks + block] = masked.astype(jnp.bfloat16)

    loop(blocks, start0)
    pl.semaphore_wait(barrier, rows)
    stripe_copy(0).start()

    def finish0(block, total):
        counts = jnp.where(depth[:, lanes(block)] == DEPTH - 1, total, 0.0)
        counts1[block] = counts
        stripe1[col * blocks + block] = counts.astype(jnp.bfloat16)

    forward_level(0, finish0)
    stripe_copy(1).start()

    def finish1(block, total):
        weight = jnp.where(depth[:, lanes(block)] == DEPTH, 1.0 / jnp.maximum(total, 1.0), 0.0)
        weights[0, block] = weight.astype(jnp.bfloat16)

    forward_level(1, finish1)

    def finish2(block, total):
        middle = depth[:, lanes(block)] == DEPTH - 1
        counts = counts1[block]
        delta = jnp.where(middle, counts * total, 0.0)
        delta1[block] = delta
        weight = jnp.where(middle, (1.0 + delta) / jnp.maximum(counts, 1.0), 0.0)
        weights[1, block] = weight.astype(jnp.bfloat16)

    backward_level(0, finish2)
    offset = (row * cols + col) * (blocks * tile)

    def finish3(block, total):
        counts0 = first[:, lanes(block)].astype(jnp.float32)
        delta = jnp.where(depth[:, lanes(block)] == DEPTH - 2, counts0 * total, 0.0)
        value = delta1[block] + delta
        dependency[:, lanes(block)] = value
        vertex = lax.broadcasted_iota(jnp.int32, value.shape, 1) + (offset + block * tile)
        kept = jnp.where(vertex != sources[...], value, 0.0)
        centrality[:, lanes(block)] = jnp.sum(kept, axis=0, keepdims=True)

    backward_level(1, finish3)

    for level in range(2):
        stripe_copy(level).wait_send()

        def sent(step, level=level):
            peer = leaving(step)
            seat_copy(code_out, code_in, code_sent, code_got, level, row, peer, peer).wait_send()
            seat_copy(
                weight_out, weight_in, weight_sent, weight_got, level, row, peer, peer
            ).wait_send()

        loop(rows - 1, sent)


def sorted_runs(keys, kinds):
    seats = keys.shape[0]
    ids = jnp.arange(seats, dtype=jnp.int32)
    ahead = jnp.logical_or(
        keys[None, :] < keys[:, None],
        jnp.logical_and(keys[None, :] == keys[:, None], ids[None, :] < ids[:, None]),
    )
    rank = jnp.sum(ahead.astype(jnp.int32), axis=1)
    placed = rank[None, :] == ids[:, None]
    order = jnp.sum(jnp.where(placed, ids[None, :], 0), axis=1)
    equal_before = jnp.logical_and(keys[None, :] == keys[:, None], ids[None, :] < ids[:, None])
    repeated = jnp.any(equal_before, axis=1)
    same = jnp.sum(jnp.where(placed, repeated[None, :], False).astype(jnp.int32), axis=1)
    kind_ids = jnp.arange(kinds, dtype=jnp.int32)
    upto = jnp.sum((keys[None, :] <= kind_ids[:, None]).astype(jnp.int32), axis=1)
    last = jnp.maximum(upto - 1, 0)
    some = jnp.any(keys[None, :] == kind_ids[:, None], axis=1).astype(jnp.int32)
    return order, same, last, some


def shards(first_counts, depth, sources, tile_pos, tile_live, tile_bits):
    batch_count, src_count, width = first_counts.shape
    row_count = lax.axis_size("row")
    col_count = lax.axis_size("col")
    tile_size = tile_bits.shape[-1]
    slot_total = tile_bits.shape[2]
    row_all = batch_count * src_count
    blocks = width // tile_size
    most = (slot_total + row_count - 1) // row_count
    seats = row_count * most
    live_count = tile_live.reshape(())
    places = tile_pos.reshape(slot_total)
    stripe_span = row_count * blocks
    row_block = places // stripe_span
    column = places % stripe_span
    owner = column // blocks
    local_block = column % blocks
    slot_ids = jnp.arange(slot_total, dtype=jnp.int32)
    before = jnp.logical_and(
        owner[:, None] == owner[None, :], slot_ids[None, :] < slot_ids[:, None]
    )
    position = owner * most + jnp.sum(before.astype(jnp.int32), axis=1)
    matched = jnp.logical_and(
        position[None, :] == jnp.arange(seats, dtype=jnp.int32)[:, None],
        slot_ids[None, :] < live_count,
    )
    filled = jnp.any(matched, axis=1)

    def seat_of(values):
        return jnp.sum(jnp.where(matched, values[None, :], 0), axis=1)

    seat_row = seat_of(row_block)
    seat_block = jnp.where(filled, seat_of(local_block), blocks)
    gathered = lax.all_gather(seat_block, "row", axis=0, tiled=False)
    arrived = lax.dynamic_slice_in_dim(
        gathered, lax.axis_index("row") * most, most, axis=1
    ).reshape(seats)
    in_runs = sorted_runs(arrived, blocks)
    row_runs = sorted_runs(seat_row, col_count * blocks)
    fields = {
        "slot": seat_of(slot_ids),
        "fill": -filled.astype(jnp.int32),
        "row": seat_row,
        "block": jnp.minimum(arrived, blocks - 1),
    }
    for prefix, runs in (("in", in_runs), ("row", row_runs)):
        for name, values in zip(("order", "same", "last", "some"), runs):
            fields[prefix + "_" + name] = values
    layout = {}
    used = 0
    for name, values in fields.items():
        layout[name] = used
        used += values.shape[0]
    table = jnp.concatenate(list(fields.values()))

    vmem = pl.BlockSpec(memory_space=pltpu.VMEM)
    block_shape = (row_all, tile_size)
    dma = pltpu.SemaphoreType.DMA
    scratch = [
        pltpu.VMEM((col_count * blocks,) + block_shape, jnp.bfloat16),
        pltpu.VMEM((col_count * blocks,) + block_shape, jnp.bfloat16),
        pltpu.VMEM((2, seats) + block_shape, jnp.int16),
        pltpu.VMEM((seats,) + block_shape, jnp.int16),
        pltpu.VMEM((seats,) + block_shape, jnp.int16),
        pltpu.VMEM((2, seats) + block_shape, jnp.bfloat16),
        pltpu.VMEM((seats,) + block_shape, jnp.bfloat16),
        pltpu.VMEM((seats,) + block_shape, jnp.bfloat16),
        pltpu.VMEM((2, blocks) + block_shape, jnp.bfloat16),
        pltpu.VMEM((blocks,) + block_shape, jnp.float32),
        pltpu.VMEM((blocks,) + block_shape, jnp.float32),
        pltpu.VMEM((seats,) + block_shape, jnp.float32),
        pltpu.VMEM((seats,) + block_shape, jnp.float32),
        pltpu.VMEM((2, blocks) + block_shape, jnp.float32),
        pltpu.VMEM((2, blocks) + block_shape, jnp.float32),
        dma((2, row_count)),
        dma((2, row_count)),
        dma((2, row_count)),
        dma((2, row_count)),
        dma((2,)),
        dma((2,)),
        dma((2,)),
        dma((2,)),
    ]
    dependency, centrality = pl.pallas_call(
        functools.partial(kernel, layout, row_count, col_count, most, blocks),
        out_shape=(
            jax.ShapeDtypeStruct((row_all, width), jnp.float32),
            jax.ShapeDtypeStruct((1, width), jnp.float32),
        ),
        in_specs=[pl.BlockSpec(memory_space=pltpu.SMEM), vmem, vmem, vmem, vmem],
        out_specs=(vmem, vmem),
        scratch_shapes=scratch,
        compiler_params=pltpu.CompilerParams(
            collective_id=0, has_side_effects=True, vmem_limit_bytes=60 * 1024 * 1024
        ),
        cost_estimate=pl.CostEstimate(
            flops=8 * seats * row_all * tile_size * tile_size,
            bytes_accessed=4 * tile_bits.size + 16 * row_all * width,
            transcendentals=4 * seats * row_all * tile_size,
        ),
    )(
        table,
        tile_bits.reshape(slot_total, tile_size // 8, tile_size),
        first_counts.reshape(row_all, width),
        depth.reshape(row_all, width),
        sources.reshape(row_all, 1),
    )
    return dependency.reshape(batch_count, src_count, width), centrality.reshape(width)


def solution(mesh):
    placed = (
        P("groups", None, ("row", "col")),
        P("groups", None, ("row", "col")),
        P("groups", None),
        P(("groups", "row"), "col", None),
        P(("groups", "row"), "col"),
        P(("groups", "row"), "col", None, None, None),
    )
    return jax.shard_map(
        shards,
        mesh=mesh,
        in_specs=placed,
        out_specs=(P("groups", None, ("row", "col")), P(("groups", "row", "col"))),
        check_vma=False,
    )
```

profile of v0, /device:TPU:31, one launch (start us, length us, event | category | flops | bytes accessed | tf_op | source)
XLA Modules:
  0.0 218.4 jit_solution(4091609576089466734)
XLA Ops:
  1.3 1.2 dynamic-slice
  3.2 0.7 and_select_fusion.1
  3.9 0.2 convert_reduce_fusion.5
  4.1 0.1 fusion.6
  4.2 0.2 select_reduce_fusion.2
  4.3 0.1 fusion.7
  4.4 0.1 convert_reduce_fusion
  4.5 0.2 fusion.9
  4.7 0.2 convert_reduce_fusion.2
  4.9 0.1 convert_reduce_fusion.1
  5.0 0.1 select_dynamic-update-slice_fusion
  5.1 0.1 reshape.195
  5.2 5.6 %all-reduce.1 = s32[8,48]{1,0:T(8,128)S(1)} all-reduce(s32[8,48]{1,0:T(8,128)S(1)} %reshape.195), channel_id=2, replica_groups=mesh['groups'=2,'row'=8,'col'=2] {'row'}, use_global_device_ids=true, to_apply=%add | all-reduce | flops 384 | bytes 3072
  10.8 0.1 constant_dynamic-slice_fusion
  10.9 0.1 reshape.188
  11.0 0.1 fusion.10
  11.1 0.1 convert_reduce_fusion.6
  11.2 0.2 fusion.8
  11.4 0.2 convert_reduce_fusion.4
  11.6 0.1 convert_reduce_fusion.3
  11.7 0.7 concatenate.3.table
  12.4 1.4 reshape.201.sources
  13.8 200.8 %shard_map.77 = (f32[32,16384]{1,0:T(8,128)}, f32[1,16384]{1,0:T(1,128)}) custom-call(s32[576]{0:T(1024)} %concatenate.3.table, s32[48,64,512]{2,1,0:T(8,128)} %bitcast.22, bf16[32,16384]{1,0:T(8,128)(2,1)} %bitcast.24, s32[32,16384]{1,0:T(8,128)} %bitcast.23, s32[32,1]{1,0:T(8,128)} %reshape.201.sources), custom_call_target="tpu_custom_call" | custom-call | flops 3221225472 | bytes 14680064 | tf_op jit(solution)/shard_map/pallas_call | solution.py:409
  214.6 0.0 copy-start
  214.6 3.1 %copy.14 = f32[2,16,16384]{2,1,0:T(8,128)} copy(f32[2,16,16384]{2,1,0:T(8,128)} %bitcast.20) | data formatting | bytes 4194304
  217.7 0.0 copy-done
  217.7 0.6 copy.15
  (9 shorter events, 0.1 us)
Async XLA Ops:
  214.6 3.1 %copy-start = (f32[1,16384]{1,0:T(1,128)S(1)}, f32[1,16384]{1,0:T(1,128)}, u32[]{:S(2)}) copy-start(f32[1,16384]{1,0:T(1,128)} %get-tuple-element.5) | copy-start | bytes 196612
where the time goes:
time: 219 us; the launch traced here: 218 us
  Pallas kernels  201 us (92%)
  local copies, waits for them, and re-layouts  7.25 us (3%)
  blocking collectives  5.62 us (3%)
  other arithmetic  2.64 us (1%)
    pallas_call x1, Pallas kernels, shards(): pl.pallas_call(functools.partial(kernel, layout, row_count, col_count, mo...  201 us
    unnamed x1, blocking collectives  5.62 us
    unnamed x6, local copies, waits for them, and re-layouts  4.96 us

commit v1 on v0

v1 whole, which is shorter than its diff:
```python
import functools

import jax
import jax.numpy as jnp
from jax import lax
from jax.experimental import pallas as pl
from jax.experimental.pallas import tpu as pltpu
from jax.sharding import PartitionSpec as P

DEPTH = 8
STEPS = 2000.0
CODE_ZERO = -32768
MESH = pl.DeviceIdType.MESH


def encode(values):
    code = (jnp.log2(jnp.maximum(values, 1.0)) * STEPS + 0.5).astype(jnp.int32) + (CODE_ZERO + 1)
    return jnp.where(values > 0.0, code, CODE_ZERO).astype(jnp.int16)


def decode(code):
    wide = code.astype(jnp.int32)
    value = jnp.exp2((wide - (CODE_ZERO + 1)).astype(jnp.float32) * (1.0 / STEPS))
    return jnp.where(wide > CODE_ZERO, value, 0.0)


def unpack(words):
    count, width = words.shape
    shifts = lax.broadcasted_iota(jnp.int32, (count, 8, width), 1)
    bits = jnp.bitwise_and(jnp.right_shift(words[:, None, :], shifts), 1)
    return bits.reshape(count * 8, width).astype(jnp.float32).astype(jnp.bfloat16)


def loop(count, body):
    def step(index, carry):
        body(index)
        return carry

    lax.fori_loop(0, count, step, 0)


def gather_kernel(rows, mine, result, landed, sent, got):
    row = lax.axis_index("row")
    barrier = pltpu.get_barrier_semaphore()

    def greet(step):
        peer = lax.rem(row + step + 1, rows)
        pl.semaphore_signal(barrier, inc=1, device_id={"row": peer}, device_id_type=MESH)

    loop(rows - 1, greet)
    pl.semaphore_wait(barrier, rows - 1)

    def copy(source, target):
        return pltpu.make_async_remote_copy(
            src_ref=mine,
            dst_ref=landed.at[source],
            send_sem=sent.at[target],
            recv_sem=got.at[source],
            device_id={"row": target},
            device_id_type=MESH,
        )

    loop(rows - 1, lambda step: copy(row, lax.rem(row + step + 1, rows)).start())
    landed[row] = mine[...]

    def arrive(step):
        peer = lax.rem(row + step + 1, rows)
        copy(peer, peer).wait_recv()

    loop(rows - 1, arrive)
    result[...] = landed[...]
    loop(rows - 1, lambda step: copy(row, lax.rem(row + step + 1, rows)).wait_send())


def gather_rows(values, rows):
    lanes = (values.shape[0] + 127) // 128 * 128
    padded = jnp.broadcast_to(jnp.pad(values, (0, lanes - values.shape[0]))[None, :], (8, lanes))
    vmem = pl.BlockSpec(memory_space=pltpu.VMEM)
    gathered = pl.pallas_call(
        functools.partial(gather_kernel, rows),
        out_shape=jax.ShapeDtypeStruct((rows, 8, lanes), values.dtype),
        in_specs=[vmem],
        out_specs=vmem,
        scratch_shapes=[
            pltpu.VMEM((rows, 8, lanes), values.dtype),
            pltpu.SemaphoreType.DMA((rows,)),
            pltpu.SemaphoreType.DMA((rows,)),
        ],
        compiler_params=pltpu.CompilerParams(collective_id=1, has_side_effects=True),
    )(padded)
    return gathered[:, 0, :]


def kernel(
    layout,
    rows,
    cols,
    most,
    blocks,
    table,
    words,
    first,
    depth,
    sources,
    dependency,
    centrality,
    stripe,
    code_out,
    code_in,
    weight_out,
    weight_in,
    weights,
    sum_out,
    sum_in,
    counts1,
    delta1,
    running,
    terms,
    code_sent,
    code_got,
    weight_sent,
    weight_got,
    stripe_sent,
    stripe_got,
    sum_sent,
    sum_got,
):
    seats = rows * most
    tile = words.shape[-1]
    half_rows = running.shape[1]
    row = lax.axis_index("row")
    col = lax.axis_index("col")
    partner = 1 - col

    def entry(name, index):
        return table[layout[name] + index]

    barrier = pltpu.get_barrier_semaphore()

    def leaving(step):
        return lax.rem(row + step + 1, rows)

    def arriving(step):
        return lax.rem(row + rows - 1 - step, rows)

    def greet(step):
        pl.semaphore_signal(barrier, inc=1, device_id={"row": leaving(step)}, device_id_type=MESH)

    loop(rows - 1, greet)
    pl.semaphore_signal(barrier, inc=1, device_id={"col": partner}, device_id_type=MESH)

    def lanes(block):
        return pl.ds(pl.multiple_of(block * tile, tile), tile)

    def view(ref, half, block):
        return ref[half * half_rows : (half + 1) * half_rows, lanes(block)]

    def tile_of(seat):
        return unpack(jnp.bitwise_and(words[entry("slot", seat)], entry("fill", seat)))

    def stripe_copy(chain, owner):
        part = pl.ds(owner * blocks, blocks)
        return pltpu.make_async_remote_copy(
            src_ref=stripe[chain].at[part],
            dst_ref=stripe[chain].at[part],
            send_sem=stripe_sent.at[chain],
            recv_sem=stripe_got.at[chain],
            device_id={"col": partner},
            device_id_type=MESH,
        )

    def seat_copy(out, into, sent, got, chain, src_row, dst_row, peer):
        return pltpu.make_async_remote_copy(
            src_ref=out[chain].at[pl.ds(dst_row * most, most)],
            dst_ref=into[chain].at[pl.ds(src_row * most, most)],
            send_sem=sent.at[chain, dst_row],
            recv_sem=got.at[chain, src_row],
            device_id={"row": peer},
            device_id_type=MESH,
        )

    def code_copy(chain, src_row, dst_row, peer):
        return seat_copy(code_out, code_in, code_sent, code_got, chain, src_row, dst_row, peer)

    def weight_copy(chain, src_row, dst_row, peer):
        return seat_copy(
            weight_out, weight_in, weight_sent, weight_got, chain, src_row, dst_row, peer
        )

    def sum_copy(chain):
        return pltpu.make_async_remote_copy(
            src_ref=sum_out[chain],
            dst_ref=sum_in[chain],
            send_sem=sum_sent.at[chain],
            recv_sem=sum_got.at[chain],
            device_id={"col": partner},
            device_id_type=MESH,
        )

    def segment_sums(load, order, same):
        def step(index, total):
            carry = total * entry(same, index).astype(jnp.float32)
            total = load(entry(order, index)) + carry
            running[index] = total
            return total

        lax.fori_loop(0, seats, step, jnp.zeros(running.shape[1:], jnp.float32))

    def segment(last, some, block):
        return running[entry(last, block)] * entry(some, block).astype(jnp.float32)

    def forward_send(chain):
        stripe_copy(chain, partner).wait_recv()

        def product(seat):
            piece = stripe[chain][entry("row", seat)]
            return encode(jnp.dot(piece, tile_of(seat), preferred_element_type=jnp.float32))

        def send(step):
            peer = leaving(step)

            def one(place):
                code_out[chain][peer * most + place] = product(peer * most + place)

            loop(most, one)
            code_copy(chain, row, peer, peer).start()

        loop(rows - 1, send)

        def own(place):
            code_in[chain][row * most + place] = product(row * most + place)

        loop(most, own)

    def forward_sum(chain, finish):
        def arrive(step):
            peer = arriving(step)
            code_copy(chain, peer, row, peer).wait_recv()

        loop(rows - 1, arrive)
        segment_sums(lambda seat: decode(code_in[chain][seat]), "in_order", "in_same")
        loop(blocks, lambda block: finish(block, segment("in_last", "in_some", block)))

    def backward_send(chain):
        def send(step):
            peer = leaving(step)

            def one(place):
                seat = peer * most + place
                weight_out[chain][seat] = weights[chain][entry("block", seat)]

            loop(most, one)
            weight_copy(chain, row, peer, peer).start()

        loop(rows - 1, send)

    def backward_sum(chain, finish):
        def product(seat, piece):
            terms[seat] = lax.dot_general(
                piece, tile_of(seat), (((1,), (1,)), ((), ())), preferred_element_type=jnp.float32
            )

        def own(place):
            seat = row * most + place
            product(seat, weights[chain][entry("block", seat)])

        loop(most, own)

        def arrive(step):
            peer = arriving(step)
            weight_copy(chain, peer, row, peer).wait_recv()

            def one(place):
                seat = peer * most + place
                product(seat, weight_in[chain][seat])

            loop(most, one)

        loop(rows - 1, arrive)
        segment_sums(lambda seat: terms[seat], "row_order", "row_same")

        def leave(block):
            sum_out[chain][block] = segment("row_last", "row_some", partner * blocks + block)

        loop(blocks, leave)
        sum_copy(chain).start()
        sum_copy(chain).wait_recv()

        def total(block):
            mine = segment("row_last", "row_some", col * blocks + block)
            finish(block, mine + sum_in[chain][block])

        loop(blocks, total)

    def start(half):
        def one(block):
            counts0 = view(first, half, block).astype(jnp.float32)
            masked = jnp.where(view(depth, half, block) == DEPTH - 2, counts0, 0.0)
            stripe[half][col * blocks + block] = masked.astype(jnp.bfloat16)

        loop(blocks, one)

    def middle_counts(half, block, total):
        counts = jnp.where(view(depth, half, block) == DEPTH - 1, total, 0.0)
        counts1[half, block] = counts
        stripe[2 + half][col * blocks + block] = counts.astype(jnp.bfloat16)

    def last_weights(half, block, total):
        last = view(depth, half, block) == DEPTH
        weight = jnp.where(last, 1.0 / jnp.maximum(total, 1.0), 0.0)
        weights[half][block] = weight.astype(jnp.bfloat16)

    def middle_weights(half, block, total):
        middle = view(depth, half, block) == DEPTH - 1
        counts = counts1[half, block]
        delta = jnp.where(middle, counts * total, 0.0)
        delta1[half, block] = delta
        weight = jnp.where(middle, (1.0 + delta) / jnp.maximum(counts, 1.0), 0.0)
        weights[2 + half][block] = weight.astype(jnp.bfloat16)

    offset = (row * cols + col) * (blocks * tile)

    def results(half, block, total):
        counts0 = view(first, half, block).astype(jnp.float32)
        delta = jnp.where(view(depth, half, block) == DEPTH - 2, counts0 * total, 0.0)
        value = delta1[half, block] + delta
        mine = slice(half * half_rows, (half + 1) * half_rows)
        dependency[mine, lanes(block)] = value
        vertex = lax.broadcasted_iota(jnp.int32, value.shape, 1) + (offset + block * tile)
        kept = jnp.where(vertex != sources[mine, :], value, 0.0)
        part = jnp.sum(kept, axis=0, keepdims=True)
        if half == 0:
            centrality[:, lanes(block)] = part
        else:
            centrality[:, lanes(block)] = centrality[:, lanes(block)] + part

    halves = (0, 1)
    for half in halves:
        start(half)
        if half == 0:
            pl.semaphore_wait(barrier, rows)
        stripe_copy(half, col).start()
    for half in halves:
        forward_send(half)
    for half in halves:
        forward_sum(half, functools.partial(middle_counts, half))
        stripe_copy(2 + half, col).start()
        forward_send(2 + half)
    for half in halves:
        forward_sum(2 + half, functools.partial(last_weights, half))
        backward_send(half)
    for half in halves:
        backward_sum(half, functools.partial(middle_weights, half))
        backward_send(2 + half)
    for half in halves:
        backward_sum(2 + half, functools.partial(results, half))

    for chain in range(4):
        stripe_copy(chain, col).wait_send()
        sum_copy(chain).wait_send()

        def sent(step, chain=chain):
            peer = leaving(step)
            code_copy(chain, row, peer, peer).wait_send()
            weight_copy(chain, row, peer, peer).wait_send()

        loop(rows - 1, sent)


def sorted_runs(keys, kinds):
    seats = keys.shape[0]
    ids = jnp.arange(seats, dtype=jnp.int32)
    ahead = jnp.logical_or(
        keys[None, :] < keys[:, None],
        jnp.logical_and(keys[None, :] == keys[:, None], ids[None, :] < ids[:, None]),
    )
    rank = jnp.sum(ahead.astype(jnp.int32), axis=1)
    placed = rank[None, :] == ids[:, None]
    order = jnp.sum(jnp.where(placed, ids[None, :], 0), axis=1)
    equal_before = jnp.logical_and(keys[None, :] == keys[:, None], ids[None, :] < ids[:, None])
    repeated = jnp.any(equal_before, axis=1)
    same = jnp.sum(jnp.where(placed, repeated[None, :], False).astype(jnp.int32), axis=1)
    kind_ids = jnp.arange(kinds, dtype=jnp.int32)
    upto = jnp.sum((keys[None, :] <= kind_ids[:, None]).astype(jnp.int32), axis=1)
    last = jnp.maximum(upto - 1, 0)
    some = jnp.any(keys[None, :] == kind_ids[:, None], axis=1).astype(jnp.int32)
    return order, same, last, some


def shards(first_counts, depth, sources, tile_pos, tile_live, tile_bits):
    batch_count, src_count, width = first_counts.shape
    row_count = lax.axis_size("row")
    col_count = lax.axis_size("col")
    tile_size = tile_bits.shape[-1]
    slot_total = tile_bits.shape[2]
    row_all = batch_count * src_count
    blocks = width // tile_size
    most = (slot_total + row_count - 1) // row_count
    seats = row_count * most
    live_count = tile_live.reshape(())
    places = tile_pos.reshape(slot_total)
    stripe_span = row_count * blocks
    row_block = places // stripe_span
    column = places % stripe_span
    owner = column // blocks
    local_block = column % blocks
    slot_ids = jnp.arange(slot_total, dtype=jnp.int32)
    before = jnp.logical_and(
        owner[:, None] == owner[None, :], slot_ids[None, :] < slot_ids[:, None]
    )
    position = owner * most + jnp.sum(before.astype(jnp.int32), axis=1)
    matched = jnp.logical_and(
        position[None, :] == jnp.arange(seats, dtype=jnp.int32)[:, None],
        slot_ids[None, :] < live_count,
    )
    filled = jnp.any(matched, axis=1)

    def seat_of(values):
        return jnp.sum(jnp.where(matched, values[None, :], 0), axis=1)

    seat_row = seat_of(row_block)
    seat_block = jnp.where(filled, seat_of(local_block), blocks)
    gathered = gather_rows(seat_block, row_count)
    arrived = lax.dynamic_slice_in_dim(
        gathered, lax.axis_index("row") * most, most, axis=1
    ).reshape(seats)
    in_runs = sorted_runs(arrived, blocks)
    row_runs = sorted_runs(seat_row, col_count * blocks)
    fields = {
        "slot": seat_of(slot_ids),
        "fill": -filled.astype(jnp.int32),
        "row": seat_row,
        "block": jnp.minimum(arrived, blocks - 1),
    }
    for prefix, runs in (("in", in_runs), ("row", row_runs)):
        for name, values in zip(("order", "same", "last", "some"), runs):
            fields[prefix + "_" + name] = values
    layout = {}
    used = 0
    for name, values in fields.items():
        layout[name] = used
        used += values.shape[0]
    table = jnp.concatenate(list(fields.values()))

    vmem = pl.BlockSpec(memory_space=pltpu.VMEM)
    half_shape = (row_all // 2, tile_size)
    dma = pltpu.SemaphoreType.DMA

    def chains(count, dtype):
        return tuple(pltpu.VMEM((count,) + half_shape, dtype) for _ in range(4))

    scratch = [
        chains(col_count * blocks, jnp.bfloat16),
        chains(seats, jnp.int16),
        chains(seats, jnp.int16),
        chains(seats, jnp.bfloat16),
        chains(seats, jnp.bfloat16),
        chains(blocks, jnp.bfloat16),
        chains(blocks, jnp.float32),
        chains(blocks, jnp.float32),
        pltpu.VMEM((2, blocks) + half_shape, jnp.float32),
        pltpu.VMEM((2, blocks) + half_shape, jnp.float32),
        pltpu.VMEM((seats,) + half_shape, jnp.float32),
        pltpu.VMEM((seats,) + half_shape, jnp.float32),
        dma((4, row_count)),
        dma((4, row_count)),
        dma((4, row_count)),
        dma((4, row_count)),
        dma((4,)),
        dma((4,)),
        dma((4,)),
        dma((4,)),
    ]
    dependency, centrality = pl.pallas_call(
        functools.partial(kernel, layout, row_count, col_count, most, blocks),
        out_shape=(
            jax.ShapeDtypeStruct((row_all, width), jnp.float32),
            jax.ShapeDtypeStruct((1, width), jnp.float32),
        ),
        in_specs=[pl.BlockSpec(memory_space=pltpu.SMEM), vmem, vmem, vmem, vmem],
        out_specs=(vmem, vmem),
        scratch_shapes=scratch,
        compiler_params=pltpu.CompilerParams(
            collective_id=0, has_side_effects=True, vmem_limit_bytes=60 * 1024 * 1024
        ),
        cost_estimate=pl.CostEstimate(
            flops=8 * seats * row_all * tile_size * tile_size,
            bytes_accessed=4 * tile_bits.size + 16 * row_all * width,
            transcendentals=4 * seats * row_all * tile_size,
        ),
    )(
        table,
        tile_bits.reshape(slot_total, tile_size // 8, tile_size),
        first_counts.reshape(row_all, width),
        depth.reshape(row_all, width),
        sources.reshape(row_all, 1),
    )
    return dependency.reshape(batch_count, src_count, width), centrality.reshape(width)


def solution(mesh):
    placed = (
        P("groups", None, ("row", "col")),
        P("groups", None, ("row", "col")),
        P("groups", None),
        P(("groups", "row"), "col", None),
        P(("groups", "row"), "col"),
        P(("groups", "row"), "col", None, None, None),
    )
    return jax.shard_map(
        shards,
        mesh=mesh,
        in_specs=placed,
        out_specs=(P("groups", None, ("row", "col")), P(("groups", "row", "col"))),
        check_vma=False,
    )
```

time: 219 us -> 200 us (0.913)
  Pallas kernels: 201 us -> 188 us
  blocking collectives: 5.62 us -> 0 us
    pallas_call x1, Pallas kernels: 201 us -> 181 us  [shards(): pl.pallas_call(functools.partial(kernel, layout, row_count, col_count, mo...]
    pallas_call x0 -> x1, Pallas kernels: none -> 6.87 us  [gather_rows(): pl.pallas_call(functools.partial(gather_kernel, rows), out_shape=jax.Shap...]
    unnamed x1 -> x0, blocking collectives: 5.62 us -> none
    unnamed x6 -> x4, local copies, waits for them, and re-layouts: 4.96 us -> 3.72 us
where the time goes in v1:
time: 200 us; the launch traced here: 199 us
  Pallas kernels  188 us (94%)
  local copies, waits for them, and re-layouts  7.3 us (4%)
  other arithmetic  2.54 us (1%)
    pallas_call x1, Pallas kernels, shards(): pl.pallas_call(functools.partial(kernel, layout, row_count, col_count, mo...  181 us
    pallas_call x1, Pallas kernels, gather_rows(): pl.pallas_call(functools.partial(gather_kernel, rows), out_shape=jax.Shap...  6.87 us

profile of v1, /device:TPU:31, one launch (start us, length us, event | category | flops | bytes accessed | tf_op | source)
XLA Modules:
  0.0 199.2 jit_solution(5081410911672244911)
XLA Ops:
  1.3 0.7 and_select_fusion.1
  2.0 0.2 convert_reduce_fusion.5
  2.2 0.1 fusion.6
  2.3 0.2 select_reduce_fusion.2
  2.5 0.1 fusion.7
  2.6 0.1 convert_reduce_fusion
  2.7 0.2 fusion.9
  2.8 0.2 convert_reduce_fusion.2
  3.0 0.1 convert_reduce_fusion.1
  3.1 0.6 broadcast_in_dim.55.mine
  3.7 1.4 reshape.187.sources
  5.1 6.9 %shard_map.77 = s32[8,8,128]{2,1,0:T(8,128)} custom-call(s32[8,128]{1,0:T(8,128)} %broadcast_in_dim.55.mine), custom_call_target="tpu_custom_call" | custom-call | tf_op jit(solution)/shard_map/pallas_call | solution.py:79
  12.0 0.8 slice.3
  12.8 0.1 dynamic-slice_reduce_fusion
  12.9 0.1 reshape.180
  12.9 0.1 fusion.10
  13.1 0.1 convert_reduce_fusion.6
  13.2 0.2 fusion.8
  13.4 0.2 convert_reduce_fusion.4
  13.6 0.1 convert_reduce_fusion.3
  13.7 0.7 concatenate.3.table
  14.4 181.1 %shard_map.78 = (f32[32,16384]{1,0:T(8,128)}, f32[1,16384]{1,0:T(1,128)}) custom-call(s32[576]{0:T(1024)} %concatenate.3.table, s32[48,64,512]{2,1,0:T(8,128)} %bitcast.21, bf16[32,16384]{1,0:T(8,128)(2,1)} %bitcast.23, s32[32,16384]{1,0:T(8,128)} %bitcast.22, s32[32,1]{1,0:T(8,128)} %reshape.187.sources), custom_call_target="tpu_custom_call" | custom-call | flops 3221225472 | bytes 14680064 | tf_op jit(solution)/shard_map/pallas_call | solution.py:474
  195.5 0.0 copy-start
  195.5 3.1 %copy.14 = f32[2,16,16384]{2,1,0:T(8,128)} copy(f32[2,16,16384]{2,1,0:T(8,128)} %bitcast.19) | data formatting | bytes 4194304
  198.6 0.0 copy-done
  198.6 0.6 copy.15
  (10 shorter events, 0.1 us)
Async XLA Ops:
  195.5 3.1 %copy-start = (f32[1,16384]{1,0:T(1,128)S(1)}, f32[1,16384]{1,0:T(1,128)}, u32[]{:S(2)}) copy-start(f32[1,16384]{1,0:T(1,128)} %get-tuple-element.5) | copy-start | bytes 196612

commit v2 on v1

--- a/solution.py
+++ b/solution.py
@@ -37,6 +37,23 @@
         return carry
 
     lax.fori_loop(0, count, step, 0)
+
+
+def divisor(count, most):
+    return max(part for part in range(1, most + 1) if count % part == 0)
+
+
+def grouped(count, size, compute, store):
+    def body(group):
+        indices = [group * size + place for place in range(size)]
+        values = [compute(index) for index in indices]
+        for index, value in zip(indices, values):
+            store(index, value)
+
+    if count == size:
+        body(0)
+    else:
+        loop(count // size, body)
 
 
 def gather_kernel(rows, mine, result, landed, sent, got):
@@ -128,6 +145,8 @@
     seats = rows * most
     tile = words.shape[-1]
     half_rows = running.shape[1]
+    several = divisor(most, 2)
+    some_blocks = divisor(blocks, 4)
     row = lax.axis_index("row")
     col = lax.axis_index("col")
     partner = 1 - col
@@ -198,13 +217,20 @@
         )
 
     def segment_sums(load, order, same):
-        def step(index, total):
-            carry = total * entry(same, index).astype(jnp.float32)
-            total = load(entry(order, index)) + carry
-            running[index] = total
+        size = divisor(seats, 8)
+
+        def group(number, total):
+            indices = [number * size + place for place in range(size)]
+            loaded = [load(entry(order, index)) for index in indices]
+            totals = []
+            for index, value in zip(indices, loaded):
+                total = total * entry(same, index).astype(jnp.float32) + value
+                totals.append(total)
+            for index, value in zip(indices, totals):
+                running[index] = value
             return total
 
-        lax.fori_loop(0, seats, step, jnp.zeros(running.shape[1:], jnp.float32))
+        lax.fori_loop(0, seats // size, group, jnp.zeros(running.shape[1:], jnp.float32))
 
     def segment(last, some, block):
         return running[entry(last, block)] * entry(some, block).astype(jnp.float32)
@@ -219,18 +245,18 @@
         def send(step):
             peer = leaving(step)
 
-            def one(place):
-                code_out[chain][peer * most + place] = product(peer * most + place)
-
-            loop(most, one)
+            def keep(place, value):
+                code_out[chain][peer * most + place] = value
+
+            grouped(most, several, lambda place: product(peer * most + place), keep)
             code_copy(chain, row, peer, peer).start()
 
         loop(rows - 1, send)
 
-        def own(place):
-            code_in[chain][row * most + place] = product(row * most + place)
-
-        loop(most, own)
+        def own(place, value):
+            code_in[chain][row * most + place] = value
+
+        grouped(most, several, lambda place: product(row * most + place), own)
 
     def forward_sum(chain, finish):
         def arrive(step):
@@ -239,66 +265,74 @@
 
         loop(rows - 1, arrive)
         segment_sums(lambda seat: decode(code_in[chain][seat]), "in_order", "in_same")
-        loop(blocks, lambda block: finish(block, segment("in_last", "in_some", block)))
+        grouped(blocks, some_blocks, lambda block: segment("in_last", "in_some", block), finish)
 
     def backward_send(chain):
+        def owned(seat):
+            return weights[chain][entry("block", seat)]
+
         def send(step):
             peer = leaving(step)
 
-            def one(place):
-                seat = peer * most + place
-                weight_out[chain][seat] = weights[chain][entry("block", seat)]
-
-            loop(most, one)
+            def keep(place, value):
+                weight_out[chain][peer * most + place] = value
+
+            grouped(most, several, lambda place: owned(peer * most + place), keep)
             weight_copy(chain, row, peer, peer).start()
 
         loop(rows - 1, send)
 
     def backward_sum(chain, finish):
         def product(seat, piece):
-            terms[seat] = lax.dot_general(
+            return lax.dot_general(
                 piece, tile_of(seat), (((1,), (1,)), ((), ())), preferred_element_type=jnp.float32
             )
 
-        def own(place):
-            seat = row * most + place
-            product(seat, weights[chain][entry("block", seat)])
-
-        loop(most, own)
+        def products(peer, piece):
+            def keep(place, value):
+                terms[peer * most + place] = value
+
+            def one(place):
+                return product(peer * most + place, piece(peer * most + place))
+
+            grouped(most, several, one, keep)
+
+        products(row, lambda seat: weights[chain][entry("block", seat)])
 
         def arrive(step):
             peer = arriving(step)
             weight_copy(chain, peer, row, peer).wait_recv()
-
-            def one(place):
-                seat = peer * most + place
-                product(seat, weight_in[chain][seat])
-
-            loop(most, one)
+            products(peer, lambda seat: weight_in[chain][seat])
 
         loop(rows - 1, arrive)
         segment_sums(lambda seat: terms[seat], "row_order", "row_same")
 
-        def leave(block):
-            sum_out[chain][block] = segment("row_last", "row_some", partner * blocks + block)
-
-        loop(blocks, leave)
+        def leaves(block):
+            return segment("row_last", "row_some", partner * blocks + block)
+
+        def leave(block, value):
+            sum_out[chain][block] = value
+
+        grouped(blocks, some_blocks, leaves, leave)
         sum_copy(chain).start()
         sum_copy(chain).wait_recv()
 
         def total(block):
             mine = segment("row_last", "row_some", col * blocks + block)
-            finish(block, mine + sum_in[chain][block])
-
-        loop(blocks, total)
+            return mine + sum_in[chain][block]
+
+        grouped(blocks, some_blocks, total, finish)
 
     def start(half):
-        def one(block):
+        def masked(block):
             counts0 = view(first, half, block).astype(jnp.float32)
-            masked = jnp.where(view(depth, half, block) == DEPTH - 2, counts0, 0.0)
-            stripe[half][col * blocks + block] = masked.astype(jnp.bfloat16)
-
-        loop(blocks, one)
+            values = jnp.where(view(depth, half, block) == DEPTH - 2, counts0, 0.0)
+            return values.astype(jnp.bfloat16)
+
+        def keep(block, value):
+            stripe[half][col * blocks + block] = value
+
+        grouped(blocks, some_blocks, masked, keep)
 
     def middle_counts(half, block, total):
         counts = jnp.where(view(depth, half, block) == DEPTH - 1, total, 0.0)

time: 200 us -> 185 us (0.925)
  Pallas kernels: 188 us -> 173 us
    pallas_call x1, Pallas kernels: 181 us -> 167 us  [shards(): pl.pallas_call(functools.partial(kernel, layout, row_count, col_count, mo...]
where the time goes in v2:
time: 185 us
  Pallas kernels  173 us (94%)
  local copies, waits for them, and re-layouts  7.3 us (4%)
  other arithmetic  2.54 us (1%)
    pallas_call x1, Pallas kernels, shards(): pl.pallas_call(functools.partial(kernel, layout, row_count, col_count, mo...  167 us
    pallas_call x1, Pallas kernels, gather_rows(): pl.pallas_call(functools.partial(gather_kernel, rows), out_shape=jax.Shap...  6.87 us
    unnamed x4, local copies, waits for them, and re-layouts  3.72 us

profile of v2, /device:TPU:31, one launch (start us, length us, event | category | flops | bytes accessed | tf_op | source)
XLA Modules:
  0.0 184.7 jit_solution(13052283722346304725)
XLA Ops:
  1.3 0.7 and_select_fusion.1
  2.0 0.2 convert_reduce_fusion.5
  2.2 0.1 fusion.6
  2.3 0.2 select_reduce_fusion.2
  2.5 0.1 fusion.7
  2.6 0.1 convert_reduce_fusion
  2.7 0.2 fusion.9
  2.8 0.2 convert_reduce_fusion.2
  3.0 0.1 convert_reduce_fusion.1
  3.1 0.6 broadcast_in_dim.55.mine
  3.7 1.4 reshape.187.sources
  5.1 6.9 %shard_map.77 = s32[8,8,128]{2,1,0:T(8,128)} custom-call(s32[8,128]{1,0:T(8,128)} %broadcast_in_dim.55.mine), custom_call_target="tpu_custom_call" | custom-call | tf_op jit(solution)/shard_map/pallas_call | solution.py:96
  12.0 0.8 slice.3
  12.8 0.1 dynamic-slice_reduce_fusion
  12.9 0.1 reshape.180
  12.9 0.1 fusion.10
  13.1 0.1 convert_reduce_fusion.6
  13.2 0.2 fusion.8
  13.4 0.2 convert_reduce_fusion.4
  13.6 0.1 convert_reduce_fusion.3
  13.7 0.7 concatenate.3.table
  14.4 166.6 %shard_map.78 = (f32[32,16384]{1,0:T(8,128)}, f32[1,16384]{1,0:T(1,128)}) custom-call(s32[576]{0:T(1024)} %concatenate.3.table, s32[48,64,512]{2,1,0:T(8,128)} %bitcast.21, bf16[32,16384]{1,0:T(8,128)(2,1)} %bitcast.23, s32[32,16384]{1,0:T(8,128)} %bitcast.22, s32[32,1]{1,0:T(8,128)} %reshape.187.sources), custom_call_target="tpu_custom_call" | custom-call | flops 3221225472 | bytes 14680064 | tf_op jit(solution)/shard_map/pallas_call | solution.py:508
  181.0 0.0 copy-start
  181.0 3.1 %copy.14 = f32[2,16,16384]{2,1,0:T(8,128)} copy(f32[2,16,16384]{2,1,0:T(8,128)} %bitcast.19) | data formatting | bytes 4194304
  184.1 0.0 copy-done
  184.1 0.6 copy.15
  (10 shorter events, 0.1 us)
Async XLA Ops:
  181.0 3.1 %copy-start = (f32[1,16384]{1,0:T(1,128)S(1)}, f32[1,16384]{1,0:T(1,128)}, u32[]{:S(2)}) copy-start(f32[1,16384]{1,0:T(1,128)} %get-tuple-element.5) | copy-start | bytes 196612

commit v3 on v2

--- a/solution.py
+++ b/solution.py
@@ -156,11 +156,14 @@
 
     barrier = pltpu.get_barrier_semaphore()
 
+    def distance(step):
+        return 1 + lax.rem(step + rows // 2 - 1, rows - 1)
+
     def leaving(step):
-        return lax.rem(row + step + 1, rows)
+        return lax.rem(row + distance(step), rows)
 
     def arriving(step):
-        return lax.rem(row + rows - 1 - step, rows)
+        return lax.rem(row + rows - distance(step), rows)
 
     def greet(step):
         pl.semaphore_signal(barrier, inc=1, device_id={"row": leaving(step)}, device_id_type=MESH)

time: 185 us -> 181 us (0.978); the launches traced: 185 us -> 179 us
  Pallas kernels: 173 us -> 168 us
    pallas_call x1, Pallas kernels: 167 us -> 161 us  [shards(): pl.pallas_call(functools.partial(kernel, layout, row_count, col_count, mo...]
where the time goes in v3:
time: 181 us; the launch traced here: 179 us
  Pallas kernels  168 us (93%)
  local copies, waits for them, and re-layouts  7.3 us (4%)
  other arithmetic  2.54 us (1%)
    pallas_call x1, Pallas kernels, shards(): pl.pallas_call(functools.partial(kernel, layout, row_count, col_count, mo...  161 us
    pallas_call x1, Pallas kernels, gather_rows(): pl.pallas_call(functools.partial(gather_kernel, rows), out_shape=jax.Shap...  6.87 us
    unnamed x4, local copies, waits for them, and re-layouts  3.72 us

profile of v3, /device:TPU:31, one launch (start us, length us, event | category | flops | bytes accessed | tf_op | source)
XLA Modules:
  0.0 178.7 jit_solution(6430832337024222268)
XLA Ops:
  1.3 0.7 and_select_fusion.1
  2.0 0.2 convert_reduce_fusion.5
  2.2 0.1 fusion.6
  2.3 0.2 select_reduce_fusion.2
  2.5 0.1 fusion.7
  2.6 0.1 convert_reduce_fusion
  2.7 0.2 fusion.9
  2.8 0.2 convert_reduce_fusion.2
  3.0 0.1 convert_reduce_fusion.1
  3.1 0.6 broadcast_in_dim.55.mine
  3.7 1.4 reshape.187.sources
  5.1 6.9 %shard_map.77 = s32[8,8,128]{2,1,0:T(8,128)} custom-call(s32[8,128]{1,0:T(8,128)} %broadcast_in_dim.55.mine), custom_call_target="tpu_custom_call" | custom-call | tf_op jit(solution)/shard_map/pallas_call | solution.py:96
  12.0 0.8 slice.3
  12.8 0.1 dynamic-slice_reduce_fusion
  12.9 0.1 reshape.180
  12.9 0.1 fusion.10
  13.1 0.1 convert_reduce_fusion.6
  13.2 0.2 fusion.8
  13.4 0.2 convert_reduce_fusion.4
  13.6 0.1 convert_reduce_fusion.3
  13.7 0.7 concatenate.3.table
  14.4 160.7 %shard_map.78 = (f32[32,16384]{1,0:T(8,128)}, f32[1,16384]{1,0:T(1,128)}) custom-call(s32[576]{0:T(1024)} %concatenate.3.table, s32[48,64,512]{2,1,0:T(8,128)} %bitcast.21, bf16[32,16384]{1,0:T(8,128)(2,1)} %bitcast.23, s32[32,16384]{1,0:T(8,128)} %bitcast.22, s32[32,1]{1,0:T(8,128)} %reshape.187.sources), custom_call_target="tpu_custom_call" | custom-call | flops 3221225472 | bytes 14680064 | tf_op jit(solution)/shard_map/pallas_call | solution.py:511
  175.0 0.0 copy-start
  175.0 3.1 %copy.14 = f32[2,16,16384]{2,1,0:T(8,128)} copy(f32[2,16,16384]{2,1,0:T(8,128)} %bitcast.19) | data formatting | bytes 4194304
  178.1 0.0 copy-done
  178.1 0.6 copy.15
  (10 shorter events, 0.1 us)
Async XLA Ops:
  175.0 3.1 %copy-start = (f32[1,16384]{1,0:T(1,128)S(1)}, f32[1,16384]{1,0:T(1,128)}, u32[]{:S(2)}) copy-start(f32[1,16384]{1,0:T(1,128)} %get-tuple-element.5) | copy-start | bytes 196612
